TPU v7x, 256 devices: a whole 4x4x8 slice. The times are simulated.
256 devices in a mesh: row: 32 (over x, z), col: 8 (over y, core).
Axes of the slice: x: 4, y: 4, z: 8, core: 2. Of those that a mesh axis runs over, the one named last changes fastest.
Arguments:
- features: bfloat16 [16384, 512], P(('row', 'col')), may hold values from -0.5 to 0.5
- slot_of_ray: int32 [16384], P(('row', 'col')), may hold values from 0 to 63
- noise: float32 [16384], P(('row', 'col')), may hold values from 0.2 to 1
Outputs:
- front: float32 [16384, 8, 2048], P('row', 'col')
- factor: float32 [16384, 1024], P('row')
All inputs are finite; a program needn't handle non-finite values.
Results may differ from a plain program's by a relative error of at most 0.0003.
Values may be sent and summed in bfloat16 or wider, within the bound.
A program may use at most 64 MiB of HBM per device.

v0:
```python
import jax
import jax.numpy as jnp
from jax import lax
from jax.sharding import PartitionSpec as P

PANEL = 256
PANELS = 4
NT = 64


def broadcast(block, axis, holder):
    block = jnp.where(lax.axis_index(axis) == holder, block, jnp.zeros_like(block))
    return lax.psum(block, axis)


def time_rate():
    length = NT / 8.0
    return 1.0 / (2.0 * length * length)


def shards(features, slot_of_ray, noise):
    ray_dev = noise.shape[0]
    col_count = lax.axis_size("col")
    row_width = ray_dev * col_count
    col_width = ray_dev * lax.axis_size("row")
    row_index = lax.axis_index("row")
    col_index = lax.axis_index("col")
    own_slots = slot_of_ray.astype(jnp.bfloat16)
    row_feat, row_slot = (
        lax.all_gather(features, "col", axis=0, tiled=True),
        lax.all_gather(own_slots, "col", axis=0, tiled=True),
    )
    col_feat, col_slot = (
        lax.all_gather(features, "row", axis=0, tiled=True),
        lax.all_gather(own_slots, "row", axis=0, tiled=True),
    )
    gram_tile = lax.dot_general(
        row_feat, col_feat, (((1,), (1,)), ((), ())), preferred_element_type=jnp.float32
    )
    slot_gap = row_slot.astype(jnp.float32)[:, None] - col_slot.astype(jnp.float32)[None, :]
    row_ray = row_index * row_width + jnp.arange(row_width, dtype=jnp.int32)
    local_cols = jnp.arange(col_width, dtype=jnp.int32)
    col_ray = (local_cols // ray_dev * col_count + col_index) * ray_dev + local_cols % ray_dev
    noise_rows = lax.dynamic_update_slice_in_dim(
        jnp.zeros((row_width,), jnp.float32), noise, col_index * ray_dev, 0
    )
    diagonal = row_ray[:, None] == col_ray[None, :]
    complement = gram_tile * jnp.exp(-slot_gap * slot_gap * time_rate()) + jnp.where(
        diagonal, noise_rows[:, None], 0.0
    )
    identity = jnp.eye(PANEL, dtype=jnp.float32)
    panel_offsets = jnp.arange(PANEL, dtype=jnp.int32)
    columns = []
    for panel_number in range(PANELS):
        panel_start = panel_number * PANEL
        owner_row = panel_start // row_width
        offset = panel_start % row_width
        block_cols = complement[:, owner_row * ray_dev : (owner_row + 1) * ray_dev]
        panel_top = complement[offset : offset + PANEL]
        diag_rows = lax.all_gather(block_cols[offset : offset + PANEL], "col", axis=1, tiled=True)
        corner = jnp.where(row_index == owner_row, diag_rows[:, offset : offset + PANEL], identity)
        triangle = jnp.linalg.cholesky(corner)
        solved = jax.scipy.linalg.solve_triangular(triangle, panel_top, lower=True)
        solved = broadcast(solved, "row", owner_row)
        mine_part = lax.dynamic_slice_in_dim(solved, row_index * ray_dev, ray_dev, 1)
        panel_cols = lax.all_gather(mine_part, "col", axis=1, tiled=True)
        complement = complement - lax.dot_general(
            panel_cols,
            solved,
            (((0,), (0,)), ((), ())),
            precision=lax.Precision.HIGHEST,
            preferred_element_type=jnp.float32,
        )
        below_mask = row_ray[:, None] >= panel_start + panel_offsets[None, :]
        columns.append(jnp.where(below_mask, panel_cols.T, 0.0))
    factor = jnp.concatenate(columns, axis=1)
    eliminated = PANELS * PANEL
    remaining = (row_ray[:, None] >= eliminated) & (col_ray[None, :] >= eliminated)
    front_out = jnp.where(remaining, complement, 0.0).reshape(row_width, 1, col_width)
    return (front_out, factor)


def solution(mesh):
    return jax.shard_map(
        shards,
        mesh=mesh,
        in_specs=(P(("row", "col"), None), P(("row", "col")), P(("row", "col"))),
        out_specs=(P("row", "col", None), P("row", None)),
        check_vma=False,
    )
```

profile of v0, /device:TPU:86, one launch (start us, length us, event | category | flops | bytes accessed | tf_op | source)
XLA Modules:
  0.0 1173.3 jit_solution(5242941656789124189)
XLA Ops:
  12.6 10.2 all-reduce.1
  23.0 63.8 %all-reduce.2 = bf16[2048]{0:T(1024)(128)(2,1)S(1)} all-reduce(bf16[2048]{0:T(1024)(128)(2,1)S(1)} %dynamic-update-slice.12), channel_id=1, replica_groups=mesh['row'=32,'col'=8] {'row'}, use_global_device_ids=true, to_apply=%add.2 | all-reduce | flops 2048 | bytes 8192
  87.8 16.4 %all_gather.36 = bf16[512,512]{1,0:T(8,128)(2,1)S(1)} all-gather(bf16[64,512]{1,0:T(8,128)(2,1)} %param.6), channel_id=1, replica_groups=mesh['row'=32,'col'=8] {'col'}, dimensions={0}, use_global_device_ids=true | all-gather | bytes 589824 | tf_op jit(solution)/shard_map/all_gather | solution.py:30
  104.1 3.9 fusion.3
  108.0 2.0 copy-done.3
  110.0 13.3 %all_gather.40 = f32[256,512]{0,1:T(8,128)S(1)} all-gather(f32[256,64]{0,1:T(8,128)S(1)} %slice.114), channel_id=1, replica_groups=mesh['row'=32,'col'=8] {'col'}, dimensions={1}, use_global_device_ids=true | all-gather | bytes 589824 | tf_op jit(solution)/shard_map/all_gather | solution.py:60
  123.5 11.7 cholesky.214
  135.3 9.8 custom-call.17
  145.6 11.7 cholesky.231
  159.6 4.3 while.8
  160.4 1.4 bitcast_dynamic-update-slice_fusion.8
  162.5 1.4 bitcast_dynamic-update-slice_fusion.8
  163.9 19.7 %custom-call.18 = f32[2,128,128]{1,2,0:T(8,128)S(1)} custom-call(f32[2,128,128]{2,1,0:T(8,128)S(1)} %get-tuple-element.30), custom_call_target="InvertDiagBlocksLowerTriangular" | custom-call | tf_op jit(solution)/shard_map/jit(_solve_triangular)/triangular_solve | solution.py:63
  183.6 2.3 fusion.10
  185.9 3.0 convolution_subtract_fusion.6
  190.0 1.5 maximum_select_fusion
  191.5 158.4 %all-reduce.8.cloned.1.call-done = f32[256,2048]{1,0:T(8,128)} async-done(((f32[256,2048]{1,0:T(8,128)}), f32[256,2048]{1,0:T(8,128)}) %all-reduce.8.cloned.1.call-update) | async-done | bytes 2097168 | tf_op jit(solution)/shard_map/psum | solution.py:13
  351.0 11.9 %all_gather.41 = f32[256,512]{0,1:T(8,128)S(1)} all-gather(f32[256,64]{0,1:T(8,128)S(1)} %copy.18), channel_id=1, replica_groups=mesh['row'=32,'col'=8] {'col'}, dimensions={1}, use_global_device_ids=true | all-gather | bytes 589824 | tf_op jit(solution)/shard_map/all_gather | solution.py:66
  362.9 11.0 convolution_subtract_fusion.2
  373.9 2.0 copy-done.1
  375.9 13.5 %all_gather.42 = f32[256,512]{0,1:T(8,128)S(1)} all-gather(f32[256,64]{0,1:T(8,128)S(1)} %slice.116), channel_id=1, replica_groups=mesh['row'=32,'col'=8] {'col'}, dimensions={1}, use_global_device_ids=true | all-gather | bytes 589824 | tf_op jit(solution)/shard_map/all_gather | solution.py:60
  389.7 11.7 cholesky.248
  402.1 9.8 custom-call.19
  412.4 11.7 cholesky.265
  426.3 4.3 while.9
  427.1 1.4 bitcast_dynamic-update-slice_fusion.9
  429.1 1.4 bitcast_dynamic-update-slice_fusion.9
  430.6 19.7 %custom-call.20 = f32[2,128,128]{1,2,0:T(8,128)S(1)} custom-call(f32[2,128,128]{2,1,0:T(8,128)S(1)} %get-tuple-element.31), custom_call_target="InvertDiagBlocksLowerTriangular" | custom-call | tf_op jit(solution)/shard_map/jit(_solve_triangular)/triangular_solve | solution.py:63
  450.2 2.3 fusion.8
  452.5 3.0 convolution_subtract_fusion.5
  456.7 1.5 maximum_select_fusion.1
  458.2 152.3 %all-reduce.10.cloned.1.call-done = f32[256,2048]{1,0:T(8,128)} async-done(((f32[256,2048]{1,0:T(8,128)}), f32[256,2048]{1,0:T(8,128)}) %all-reduce.10.cloned.1.call-update) | async-done | bytes 2097168 | tf_op jit(solution)/shard_map/psum | solution.py:13
  611.6 11.9 %all_gather.43 = f32[256,512]{0,1:T(8,128)S(1)} all-gather(f32[256,64]{0,1:T(8,128)S(1)} %copy.21), channel_id=1, replica_groups=mesh['row'=32,'col'=8] {'col'}, dimensions={1}, use_global_device_ids=true | all-gather | bytes 589824 | tf_op jit(solution)/shard_map/all_gather | solution.py:66
  623.5 11.0 convolution_subtract_fusion.1
  634.6 2.0 copy-done.2
  636.6 13.3 %all_gather.44 = f32[256,512]{0,1:T(8,128)S(1)} all-gather(f32[256,64]{0,1:T(8,128)S(1)} %slice.118), channel_id=1, replica_groups=mesh['row'=32,'col'=8] {'col'}, dimensions={1}, use_global_device_ids=true | all-gather | bytes 589824 | tf_op jit(solution)/shard_map/all_gather | solution.py:60
  650.1 11.7 cholesky.282
  662.5 9.8 custom-call.21
  672.8 11.7 cholesky.299
  686.7 4.5 while.10
  687.7 1.4 bitcast_dynamic-update-slice_fusion.10
  689.8 1.4 bitcast_dynamic-update-slice_fusion.10
  691.2 19.7 %custom-call.22 = f32[2,128,128]{1,2,0:T(8,128)S(1)} custom-call(f32[2,128,128]{2,1,0:T(8,128)S(1)} %get-tuple-element.32), custom_call_target="InvertDiagBlocksLowerTriangular" | custom-call | tf_op jit(solution)/shard_map/jit(_solve_triangular)/triangular_solve | solution.py:63
  710.9 2.3 fusion.6
  713.2 3.0 convolution_subtract_fusion.4
  717.3 1.5 maximum_select_fusion.2
  718.9 152.3 %all-reduce.12.cloned.1.call-done = f32[256,2048]{1,0:T(8,128)} async-done(((f32[256,2048]{1,0:T(8,128)}), f32[256,2048]{1,0:T(8,128)}) %all-reduce.12.cloned.1.call-update) | async-done | bytes 2097168 | tf_op jit(solution)/shard_map/psum | solution.py:13
  872.3 11.9 %all_gather.45 = f32[256,512]{0,1:T(8,128)S(1)} all-gather(f32[256,64]{0,1:T(8,128)S(1)} %copy.24), channel_id=1, replica_groups=mesh['row'=32,'col'=8] {'col'}, dimensions={1}, use_global_device_ids=true | all-gather | bytes 589824 | tf_op jit(solution)/shard_map/all_gather | solution.py:66
  884.2 11.0 convolution_subtract_fusion
  895.2 2.0 copy-done
  897.2 13.3 %all_gather.46 = f32[256,512]{0,1:T(8,128)S(1)} all-gather(f32[256,64]{0,1:T(8,128)S(1)} %slice.120), channel_id=1, replica_groups=mesh['row'=32,'col'=8] {'col'}, dimensions={1}, use_global_device_ids=true | all-gather | bytes 589824 | tf_op jit(solution)/shard_map/all_gather | solution.py:60
  910.7 11.7 cholesky.316
  923.1 9.8 custom-call.23
  933.4 11.7 cholesky.333
  947.3 4.3 while.11
  951.6 19.7 %custom-call.24 = f32[2,128,128]{1,2,0:T(8,128)S(1)} custom-call(f32[2,128,128]{2,1,0:T(8,128)S(1)} %get-tuple-element.33), custom_call_target="InvertDiagBlocksLowerTriangular" | custom-call | tf_op jit(solution)/shard_map/jit(_solve_triangular)/triangular_solve | solution.py:63
  971.3 2.3 fusion.4
  973.6 3.0 convolution_subtract_fusion.3
  977.7 1.5 maximum_select_fusion.3
  979.3 152.3 %all-reduce.14.cloned.1.call-done = f32[256,2048]{1,0:T(8,128)} async-done(((f32[256,2048]{1,0:T(8,128)}), f32[256,2048]{1,0:T(8,128)}) %all-reduce.14.cloned.1.call-update) | async-done | bytes 2097168 | tf_op jit(solution)/shard_map/psum | solution.py:13
  1132.7 11.9 %all_gather.47 = f32[256,512]{0,1:T(8,128)S(1)} all-gather(f32[256,64]{0,1:T(8,128)S(1)} %copy.27), channel_id=1, replica_groups=mesh['row'=32,'col'=8] {'col'}, dimensions={1}, use_global_device_ids=true | all-gather | bytes 589824 | tf_op jit(solution)/shard_map/all_gather | solution.py:66
  1144.6 9.3 select_bitcast_fusion
  1153.9 10.9 copy.29
  1165.0 1.6 pad_maximum_fusion
  (120 shorter events, 30.1 us)
Async XLA Ops:
  7.2 97.0 %all-gather.2.cloned.1.call-start = ((), (), s32[]{:S(2)}) async-start(), calls=%async_computation | async-start | bytes 2162688 | tf_op jit(solution)/shard_map/all_gather | solution.py:34
  7.9 342.0 %all-reduce.8.cloned.1.call-start = ((), (), s32[]{:S(2)}) async-start(), calls=%async_computation.1 | async-start | bytes 4194304 | tf_op jit(solution)/shard_map/psum | solution.py:13
  108.0 2.0 copy-start.3
  191.5 419.0 %all-reduce.10.cloned.1.call-start = ((), (), s32[]{:S(2)}) async-start(), calls=%async_computation.2 | async-start | bytes 4194304 | tf_op jit(solution)/shard_map/psum | solution.py:13
  373.9 2.0 copy-start.1
  458.2 413.0 %all-reduce.12.cloned.1.call-start = ((), (), s32[]{:S(2)}) async-start(), calls=%async_computation.3 | async-start | bytes 4194304 | tf_op jit(solution)/shard_map/psum | solution.py:13
  634.6 2.0 copy-start.2
  718.8 412.8 %all-reduce.14.cloned.1.call-start = ((), (), s32[]{:S(2)}) async-start(), calls=%async_computation.4 | async-start | bytes 4194304 | tf_op jit(solution)/shard_map/psum | solution.py:13
  895.2 2.0 copy-start
Sparse Core Ops, SparseCore 0:
  10.6 77.6 all-gather.1
  191.6 158.2 all-reduce.7
  458.3 152.2 all-reduce.9
  718.9 152.2 all-reduce.11
  979.4 152.2 all-reduce.13
where the time goes:
time: 1180 us; the launch traced here: 1170 us
  waiting for transfers between devices  616 us (52%)
  other arithmetic  226 us (19%)
  blocking collectives  191 us (16%)
  matrix products  73.7 us (6%)
  local copies, waits for them, and re-layouts  44 us (4%)
  between operations  21.3 us (2%)
    psum x4, waiting for transfers between devices, broadcast(): return lax.psum(block, axis)  615 us
    another operation x27, other arithmetic, shards(): triangle = jnp.linalg.cholesky(corner)  138 us
    another operation x9, other arithmetic, shards(): solved = jax.scipy.linalg.solve_triangular(triangle, panel_top, lower=True)  78.8 us
    unnamed x2, blocking collectives  74 us
    all_gather x4, blocking collectives, shards(): lax.all_gather(block_cols[offset:offset + PANEL], 'col', axis=1, tiled=True)  53.3 us
    all_gather x4, blocking collectives, shards(): panel_cols = lax.all_gather(mine_part, 'col', axis=1, tiled=True)  47.6 us
    dot_general x4, matrix products, shards(): lax.dot_general(panel_cols, solved, (((0,), (0,)), ((), ())), precision=l...  42.3 us
    another operation x12, matrix products, shards(): solved = jax.scipy.linalg.solve_triangular(triangle, panel_top, lower=True)  25.6 us
  transfers between devices with their start and end apart: 5, of which 4 were waited for; matrix products, arithmetic and copies ran while one was open for 0% of the time, Pallas kernels for 0%

commit v1 on v0

v1 whole, which is shorter than its diff:
```python
import functools

import jax
import jax.numpy as jnp
from jax import lax
from jax.experimental import pallas as pl
from jax.experimental.pallas import tpu as pltpu
from jax.sharding import PartitionSpec as P

PANEL = 256
PANELS = 4
NT = 64
HEAD = PANEL * PANELS
EXTRA = 128
W = 8
B = 128
MESH = pl.DeviceIdType.MESH
HIGHEST = lax.Precision.HIGHEST
F32 = jnp.float32
BF16 = jnp.bfloat16
VMEM = pl.BlockSpec(memory_space=pltpu.VMEM)
ANY = pl.BlockSpec(memory_space=pl.ANY)


def time_rate():
    length = NT / 8.0
    return 1.0 / (2.0 * length * length)


def nn(a, b, precision=None):
    return lax.dot_general(a, b, (((1,), (0,)), ((), ())), precision=precision, preferred_element_type=F32)


def nt(a, b, precision=None):
    return lax.dot_general(a, b, (((1,), (1,)), ((), ())), precision=precision, preferred_element_type=F32)


def tn(a, b, precision=None):
    return lax.dot_general(a, b, (((0,), (0,)), ((), ())), precision=precision, preferred_element_type=F32)


def split(x):
    hi = x.astype(BF16)
    return hi, (x - hi.astype(F32)).astype(BF16)


def gather_kernel(n_row, n_col, pay_ref, col_ref, row_ref, head_ref, local_sem, csend, crecv, rsend, rrecv, hsend, hrecv):
    r, c = lax.axis_index("row"), lax.axis_index("col")
    rays = pay_ref.shape[0]

    barrier = pltpu.get_barrier_semaphore()
    for d in range(1, n_row):
        pl.semaphore_signal(barrier, inc=1, device_id=(lax.rem(r + d, n_row), c), device_id_type=MESH)
    for d in range(1, n_col):
        pl.semaphore_signal(barrier, inc=1, device_id=(r, lax.rem(c + d, n_col)), device_id_type=MESH)
    pl.semaphore_wait(barrier, n_row + n_col - 2)

    def to_rows(d, src_row):
        return pltpu.make_async_remote_copy(
            src_ref=pay_ref,
            dst_ref=col_ref.at[src_row],
            send_sem=csend.at[d],
            recv_sem=crecv.at[src_row],
            device_id=(lax.rem(r + d, n_row), c),
            device_id_type=MESH,
        )

    def to_cols(d, src_col):
        return pltpu.make_async_remote_copy(
            src_ref=pay_ref,
            dst_ref=row_ref.at[src_col],
            send_sem=rsend.at[d],
            recv_sem=rrecv.at[src_col],
            device_id=(r, lax.rem(c + d, n_col)),
            device_id_type=MESH,
        )

    def head_to_cols(d, src_col):
        return pltpu.make_async_remote_copy(
            src_ref=col_ref.at[pl.ds(0, 2)],
            dst_ref=head_ref.at[:, pl.ds(pl.multiple_of(src_col * rays, rays), rays)],
            send_sem=hsend.at[d],
            recv_sem=hrecv.at[src_col],
            device_id=(r, lax.rem(c + d, n_col)),
            device_id_type=MESH,
        )

    @pl.when(r < 2)
    def _():
        for d in range(1, n_row):
            to_rows(d, r).start()

    own = pltpu.make_async_copy(pay_ref, col_ref.at[r], local_sem.at[0])
    own.start()
    own_row = pltpu.make_async_copy(pay_ref, row_ref.at[c], local_sem.at[1])
    own_row.start()
    own.wait()
    for s in range(2):
        @pl.when(r != s)
        def _(s=s):
            to_rows(1, s).wait_recv()

    for d in range(1, n_col):
        head_to_cols(d, c).start()
    own_head = pltpu.make_async_copy(
        col_ref.at[pl.ds(0, 2)], head_ref.at[:, pl.ds(pl.multiple_of(c * rays, rays), rays)], local_sem.at[2]
    )
    own_head.start()

    @pl.when(r >= 2)
    def _():
        for d in range(1, n_row):
            to_rows(d, r).start()

    for d in range(1, n_col):
        to_cols(d, c).start()

    own_row.wait()
    own_head.wait()
    for d in range(1, n_col):
        head_to_cols(d, lax.rem(c + d, n_col)).wait_recv()
        to_cols(d, lax.rem(c + d, n_col)).wait_recv()
    for s in range(2, n_row):
        @pl.when(r != s)
        def _(s=s):
            to_rows(1, s).wait_recv()
    for d in range(1, n_col):
        head_to_cols(d, c).wait_send()
        to_cols(d, c).wait_send()
    for d in range(1, n_row):
        to_rows(d, r).wait_send()


def gather(payload, n_row, n_col):
    rays, width = payload.shape
    dma = pltpu.SemaphoreType.DMA
    return pl.pallas_call(
        functools.partial(gather_kernel, n_row, n_col),
        out_shape=(
            jax.ShapeDtypeStruct((n_row, rays, width), BF16),
            jax.ShapeDtypeStruct((n_col, rays, width), BF16),
            jax.ShapeDtypeStruct((2, n_col * rays, width), BF16),
        ),
        in_specs=[ANY],
        out_specs=(ANY, ANY, ANY),
        scratch_shapes=[
            dma((3,)), dma((n_row,)), dma((n_row,)), dma((n_col,)), dma((n_col,)), dma((n_col,)), dma((n_col,)),
        ],
        compiler_params=pltpu.CompilerParams(collective_id=0, has_side_effects=True),
        name="gather_features",
    )(payload)


def table():
    s = lax.broadcasted_iota(jnp.int32, (EXTRA, 512), 0)
    q = lax.broadcasted_iota(jnp.int32, (EXTRA, 512), 1)
    part = q // NT
    gap = (s - q % NT).astype(F32)
    value = jnp.exp(-gap * gap * time_rate())
    hi = value.astype(BF16).astype(F32)
    mid = (value - hi).astype(BF16).astype(F32)
    low = value - hi - mid
    kernel_part = jnp.where(part == 0, hi, jnp.where(part == 1, mid, jnp.where(part == 2, low, 0.0)))
    chosen = jnp.where(part < 4, kernel_part, jnp.where(gap == 0.0, 1.0, 0.0))
    return jnp.where(s < NT, chosen, 0.0).astype(BF16)


def lookups(extra, tab):
    both = nn(extra, tab).astype(BF16)
    return both[:, :256], both[:, 256:]


def noise_of(extra):
    e = extra[:, NT : NT + 3].astype(F32)
    return (e[:, 0:1] + e[:, 1:2]) + e[:, 2:3]


def factor_block(d_ref):
    lane = lax.broadcasted_iota(jnp.int32, (W, B), 1)
    sub = lax.broadcasted_iota(jnp.int32, (W, B), 0)

    def row(x, i):
        return jnp.broadcast_to(x[i : i + 1, :], (W, B))

    def col(x, i):
        return jnp.broadcast_to(x[:, i : i + 1], (W, B))

    for k in range(B // W):
        lo = W * k
        rows = d_ref[lo : lo + W, :]
        cols = [col(rows, lo + i) for i in range(W)]
        inside = (lane >= lo) & (lane < lo + W)
        rows = jnp.where(inside, jnp.where(lane - lo == sub, 1.0, 0.0), rows)
        done = jnp.zeros((W, B), F32)
        for i in range(W):
            pivot = row(cols[i], i)
            inverse = 1.0 / pivot
            current = row(rows, i)
            done = jnp.where(sub == i, current * lax.rsqrt(pivot), done)
            scaled = current * inverse
            rows = jnp.where(sub == i, scaled, rows - cols[i] * scaled)
            for j in range(i + 1, W):
                entry = row(cols[j], i) * inverse
                cols[j] = jnp.where(sub == i, entry, cols[j] - cols[i] * entry)
        d_ref[lo : lo + W, :] = done
        spread = [row(rows, i) for i in range(W)]
        for m in range(k + 1, B // W):
            other = d_ref[W * m : W * m + W, :]
            total = jnp.where(inside, 0.0, other)
            for i in range(W):
                total = total - col(other, lo + i) * spread[i]
            d_ref[W * m : W * m + W, :] = total


def head_kernel(head_ref, uhi_ref, ulo_ref, whi_ref, wlo_ref, s_ref, w_ref, d_ref):
    n = HEAD // B
    feat = head_ref[:, : head_ref.shape[1] - EXTRA]
    extra = head_ref[:, head_ref.shape[1] - EXTRA :]
    value, hot = lookups(extra, table())
    noise = noise_of(extra)
    for i in range(n):
        rs = slice(B * i, B * i + B)
        rr = lax.broadcasted_iota(jnp.int32, (B, HEAD - B * i), 0)
        cc = lax.broadcasted_iota(jnp.int32, (B, HEAD - B * i), 1)
        s_ref[rs, B * i :] = nt(feat[rs], feat[B * i :]) * nt(value[rs], hot[B * i :]) + jnp.where(rr == cc, noise[rs], 0.0)

    r = lax.broadcasted_iota(jnp.int32, (B, B), 0)
    c = lax.broadcasted_iota(jnp.int32, (B, B), 1)

    def tail(j):
        def go():
            lo = B * (j + 1)
            if lo >= HEAD:
                return
            solved = nn(w_ref[j], s_ref[lo - B : lo, lo:], HIGHEST)
            s_ref[lo - B : lo, lo:] = solved
            uhi_ref[lo - B : lo, lo:], ulo_ref[lo - B : lo, lo:] = split(solved)
            for i in range(j + 1, n):
                at = B * (i - j - 1)
                s_ref[B * i : B * i + B, B * i :] -= tn(solved[:, at : at + B], solved[:, at:], HIGHEST)

        return go

    def step(j, carry):
        at = pl.multiple_of(j * B, B)
        d_ref[...] = s_ref[pl.ds(at, B), pl.ds(at, B)]
        factor_block(d_ref)
        w_ref[j] = jnp.where(r >= c, d_ref[...], 0.0)
        lax.switch(j, [tail(i) for i in range(n)])
        return carry

    lax.fori_loop(0, n, step, 0)
    for p in range(PANELS):
        a, b = w_ref[2 * p], w_ref[2 * p + 1]
        low = -nn(b, tn(s_ref[PANEL * p : PANEL * p + B, PANEL * p + B : PANEL * p + PANEL], a, HIGHEST), HIGHEST)
        for x, rs, cs in ((a, slice(0, B), slice(0, B)), (low, slice(B, PANEL), slice(0, B)), (b, slice(B, PANEL), slice(B, PANEL))):
            whi_ref[p, rs, cs], wlo_ref[p, rs, cs] = split(x)
        whi_ref[p, :B, B:] = jnp.zeros((B, B), BF16)
        wlo_ref[p, :B, B:] = jnp.zeros((B, B), BF16)


def factor_head(head):
    return pl.pallas_call(
        head_kernel,
        out_shape=(
            jax.ShapeDtypeStruct((HEAD, HEAD), BF16),
            jax.ShapeDtypeStruct((HEAD, HEAD), BF16),
            jax.ShapeDtypeStruct((PANELS, PANEL, PANEL), BF16),
            jax.ShapeDtypeStruct((PANELS, PANEL, PANEL), BF16),
        ),
        in_specs=[VMEM],
        out_specs=(VMEM,) * 4,
        scratch_shapes=[pltpu.VMEM((HEAD, HEAD), F32), pltpu.VMEM((HEAD // B, B, B), F32), pltpu.VMEM((B, B), F32)],
        compiler_params=pltpu.CompilerParams(vmem_limit_bytes=40 << 20),
        name="factor_head",
    )(head)


def front_kernel(row_ref, head_ref, col_ref, uhi_ref, ulo_ref, whi_ref, wlo_ref, front_ref, factor_ref, tab_ref, hhot_ref, rval_ref, rhi_ref, rlo_ref, hi_ref, lo_ref):
    step = pl.program_id(0)
    r, c = lax.axis_index("row"), lax.axis_index("col")
    f = head_ref.shape[1] - EXTRA
    rows = row_ref.shape[0]
    tile = col_ref.shape[0]
    rays = rows // lax.axis_size("col")

    def solve(ref, value, noise, hi_out, lo_out):
        feat = ref[:, :f]
        n = ref.shape[0]
        for p in range(PANELS):
            ps = slice(PANEL * p, PANEL * p + PANEL)
            x = nt(feat, head_ref[ps, :f]) * nt(value, hhot_ref[ps])
            if noise is not None:
                rr = r * n + lax.broadcasted_iota(jnp.int32, (n, PANEL), 0)
                cc = PANEL * p + lax.broadcasted_iota(jnp.int32, (n, PANEL), 1)
                x = x + jnp.where(rr == cc, noise, 0.0)
            if p > 0:
                k = PANEL * p
                x = x - (nn(hi_out[:, :k], uhi_ref[:k, ps]) + (nn(hi_out[:, :k], ulo_ref[:k, ps]) + nn(lo_out[:, :k], uhi_ref[:k, ps])))
            xh, xl = split(x)
            s = nt(xh, whi_ref[p]) + (nt(xh, wlo_ref[p]) + nt(xl, whi_ref[p]))
            hi_out[:, ps], lo_out[:, ps] = split(s)
            if noise is not None:
                factor_ref[:, ps] = jnp.where(rr >= cc, s, 0.0)

    @pl.when(step == 0)
    def _():
        tab_ref[...] = table()
        hhot_ref[...] = lookups(head_ref[:, f:], tab_ref[...])[1]
        rval_ref[...] = lookups(row_ref[:, f:], tab_ref[...])[0]
        solve(row_ref, rval_ref[...], noise_of(row_ref[:, f:]), rhi_ref, rlo_ref)

    value, hot = lookups(col_ref[:, f:], tab_ref[...])
    solve(col_ref, value, None, hi_ref, lo_ref)
    full = nt(row_ref[:, :f], col_ref[:, :f]) * nt(rval_ref[...], hot)
    ri = lax.broadcasted_iota(jnp.int32, (rows, tile), 0)
    li = step * tile + lax.broadcasted_iota(jnp.int32, (rows, tile), 1)
    col_local = li - r * rays
    full = full + jnp.where(ri - c * rays == col_local, jnp.where((col_local >= 0) & (col_local < rays), noise_of(row_ref[:, f:]), 0.0), 0.0)
    full = full - (nt(rhi_ref[...], hi_ref[...]) + (nt(rhi_ref[...], lo_ref[...]) + nt(rlo_ref[...], hi_ref[...])))
    first = jnp.where(r >= HEAD // rows, HEAD // (rows // rays * rays) * rays, tile * pl.num_programs(0))
    front_ref[:, 0, :] = jnp.where(li >= first, full, 0.0)


def front_and_factor(row, head, col, uhi, ulo, whi, wlo):
    rows, width = row.shape
    cols = col.shape[0]
    tile = 512
    whole = lambda a: pl.BlockSpec(a.shape, lambda i: (0,) * a.ndim)
    return pl.pallas_call(
        front_kernel,
        grid=(cols // tile,),
        out_shape=(jax.ShapeDtypeStruct((rows, 1, cols), F32), jax.ShapeDtypeStruct((rows, HEAD), F32)),
        in_specs=[whole(row), whole(head), pl.BlockSpec((tile, width), lambda i: (i, 0)), whole(uhi), whole(ulo), whole(whi), whole(wlo)],
        out_specs=(pl.BlockSpec((rows, 1, tile), lambda i: (0, 0, i)), pl.BlockSpec((rows, HEAD), lambda i: (0, 0))),
        scratch_shapes=[
            pltpu.VMEM((EXTRA, 512), BF16),
            pltpu.VMEM((HEAD, 256), BF16),
            pltpu.VMEM((rows, 256), BF16),
            pltpu.VMEM((rows, HEAD), BF16),
            pltpu.VMEM((rows, HEAD), BF16),
            pltpu.VMEM((tile, HEAD), BF16),
            pltpu.VMEM((tile, HEAD), BF16),
        ],
        compiler_params=pltpu.CompilerParams(vmem_limit_bytes=56 << 20),
        name="front_and_factor",
    )(row, head, col, uhi, ulo, whi, wlo)


def shards(features, slot_of_ray, noise):
    n_row, n_col = lax.axis_size("row"), lax.axis_size("col")
    rays = noise.shape[0]
    lanes = jnp.arange(EXTRA, dtype=jnp.int32)[None, :]
    hi = noise.astype(BF16).astype(F32)
    mid = (noise - hi).astype(BF16).astype(F32)
    low = noise - hi - mid
    extra = jnp.where(lanes == slot_of_ray[:, None], 1.0, 0.0)
    for i, part in enumerate((hi, mid, low)):
        extra = jnp.where(lanes == NT + i, part[:, None], extra)
    payload = jnp.concatenate([features, extra.astype(BF16)], axis=1)
    width = payload.shape[1]
    col, row, head = gather(payload, n_row, n_col)
    col, row, head = col.reshape(n_row * rays, width), row.reshape(n_col * rays, width), head.reshape(HEAD, width)
    return front_and_factor(row, head, col, *factor_head(head))


def solution(mesh):
    return jax.shard_map(
        shards,
        mesh=mesh,
        in_specs=(P(("row", "col"), None), P(("row", "col")), P(("row", "col"))),
        out_specs=(P("row", "col", None), P("row", None)),
        check_vma=False,
    )
```

time: 1180 us -> 220 us (0.19)
  waiting for transfers between devices: 616 us -> 0 us
  other arithmetic: 226 us -> 3.71 us
  Pallas kernels: 0 us -> 210 us
  blocking collectives: 191 us -> 0 us
  matrix products: 73.7 us -> 0 us
  local copies, waits for them, and re-layouts: 44 us -> 5.69 us
  between operations: 21.3 us -> 0.67 us
    psum x4 -> x0, waiting for transfers between devices: 615 us -> none  [broadcast(): return lax.psum(block, axis)]
    another operation x36 -> x0, other arithmetic: 217 us -> none  [the longest x27 138 us: shards(): triangle = jnp.linalg.cholesky(corner)]
    pallas_call x0 -> x3, Pallas kernels: none -> 210 us  [the longest x1 126 us: gather(): pl.pallas_call(functools.partial(gather_kernel, n_row, n_col), out_shape=...]
    all_gather x9 -> x0, blocking collectives: 117 us -> none  [the longest x4 53.3 us: shards(): lax.all_gather(block_cols[offset:offset + PANEL], 'col', axis=1, tiled=True)]
    unnamed x2 -> x0, blocking collectives: 74 us -> none
    dot_general x5 -> x0, matrix products: 46.2 us -> none  [the longest x4 42.3 us: shards(): lax.dot_general(panel_cols, solved, (((0,), (0,)), ((), ())), precision=l...]
    another operation x20 -> x0, matrix products: 27.5 us -> none  [the longest x12 25.6 us: shards(): solved = jax.scipy.linalg.solve_triangular(triangle, panel_top, lower=True)]
    another operation x37 -> x0, local copies, waits for them, and re-layouts: 16.4 us -> none  [the longest x29 16.3 us: shards(): solved = jax.scipy.linalg.solve_triangular(triangle, panel_top, lower=True)]
  transfers between devices with their start and end apart: 5 -> 0, of which waited for: 4 -> 0; matrix products, arithmetic and copies ran while one was open for 0% -> 0% of each run, Pallas kernels for 0% -> 0%
where the time goes in v1:
time: 220 us
  Pallas kernels  210 us (95%)
  local copies, waits for them, and re-layouts  5.69 us (3%)
  other arithmetic  3.71 us (2%)
    pallas_call x1, Pallas kernels, gather(): pl.pallas_call(functools.partial(gather_kernel, n_row, n_col), out_shape=...  126 us
    pallas_call x1, Pallas kernels, factor_head(): pl.pallas_call(head_kernel, out_shape=(jax.ShapeDtypeStruct((HEAD, HEAD),...  47.2 us
    pallas_call x1, Pallas kernels, front_and_factor(): pl.pallas_call(front_kernel, grid=(cols // tile,), out_shape=(jax.ShapeDt...  37.2 us
    unnamed x10, local copies, waits for them, and re-layouts  5.69 us

profile of v1, /device:TPU:86, one launch (start us, length us, event | category | flops | bytes accessed | tf_op | source)
XLA Modules:
  0.0 220.3 jit_solution(14277809063217601873)
XLA Ops:
  0.6 0.7 fusion.1
  1.4 0.7 convert_convert_fusion
  2.1 0.7 select_convert_fusion
  2.9 1.5 pad_maximum_fusion.pay_ref
  4.3 125.8 %gather_features.1 = (bf16[32,64,640]{2,1,0:T(8,128)(2,1)}, bf16[8,64,640]{2,1,0:T(8,128)(2,1)}, bf16[2,512,640]{2,1,0:T(8,128)(2,1)}) custom-call(bf16[64,640]{1,0:T(8,128)(2,1)} %pad_maximum_fusion.pay_ref), custom_call_target="tpu_custom_call" | custom-call | tf_op jit(solution)/shard_map/gather_features/pallas_call | solution.py:137
  130.2 0.0 copy-start
  130.2 1.3 copy-done
  131.5 47.2 %factor_head.1 = (bf16[1024,1024]{1,0:T(8,128)(2,1)S(1)}, bf16[1024,1024]{1,0:T(8,128)(2,1)S(1)}, bf16[4,256,256]{2,1,0:T(8,128)(2,1)S(1)}, bf16[4,256,256]{2,1,0:T(8,128)(2,1)S(1)}) custom-call(bf16[1024,640]{1,0:T(8,128)(2,1)S(1)} %bitcast.4), custom_call_target="tpu_custom_call" | custom-call | tf_op jit(solution)/shard_map/factor_head/pallas_call | solution.py:263
  178.7 0.0 copy-start.1
  178.7 1.3 copy-done.1
  180.0 0.0 copy-start.2
  180.0 1.4 copy-done.2
  181.4 0.0 copy-start.3
  181.4 0.9 copy-done.3
  182.3 0.0 copy-start.4
  182.3 0.8 copy-done.4
  183.1 37.2 %front_and_factor.1 = (f32[512,1,2048]{2,1,0:T(1,128)}, f32[512,1024]{1,0:T(8,128)}) custom-call(bf16[512,640]{1,0:T(8,128)(2,1)} %bitcast.6, bf16[1024,640]{1,0:T(8,128)(2,1)} %bitcast.3, bf16[2048,640]{1,0:T(8,128)(2,1)} %bitcast.5, bf16[1024,1024]{1,0:T(8,128)(2,1)} %copy-done.1, bf16[1024,1024]{1,0:T(8,128)(2,1)} %copy-done.2, ...), custom_call_target="tpu_custom_call" | custom-call | tf_op jit(solution)/shard_map/front_and_factor/pallas_call | solution.py:330
  (2 shorter events, 0.0 us)
Async XLA Ops:
  130.2 1.3 copy-start
  178.7 1.3 copy-start.1
  180.0 1.4 copy-start.2
  181.4 0.9 copy-start.3
  182.3 0.8 copy-start.4

commit v2 on v1

--- a/solution.py
+++ b/solution.py
@@ -44,111 +44,159 @@
     return hi, (x - hi.astype(F32)).astype(BF16)
 
 
-def gather_kernel(n_row, n_col, pay_ref, col_ref, row_ref, head_ref, local_sem, csend, crecv, rsend, rrecv, hsend, hrecv):
-    r, c = lax.axis_index("row"), lax.axis_index("col")
-    rays = pay_ref.shape[0]
-
-    barrier = pltpu.get_barrier_semaphore()
-    for d in range(1, n_row):
-        pl.semaphore_signal(barrier, inc=1, device_id=(lax.rem(r + d, n_row), c), device_id_type=MESH)
-    for d in range(1, n_col):
-        pl.semaphore_signal(barrier, inc=1, device_id=(r, lax.rem(c + d, n_col)), device_id_type=MESH)
-    pl.semaphore_wait(barrier, n_row + n_col - 2)
-
-    def to_rows(d, src_row):
-        return pltpu.make_async_remote_copy(
-            src_ref=pay_ref,
-            dst_ref=col_ref.at[src_row],
-            send_sem=csend.at[d],
-            recv_sem=crecv.at[src_row],
-            device_id=(lax.rem(r + d, n_row), c),
-            device_id_type=MESH,
+NX, NZ = 4, 8
+QUARTERS = 4
+
+
+def remote(src, dst, send_sem, recv_sem, device):
+    return pltpu.make_async_remote_copy(
+        src_ref=src, dst_ref=dst, send_sem=send_sem, recv_sem=recv_sem, device_id=device, device_id_type=MESH
+    )
+
+
+class Feed:
+    def __init__(self, n_row, n_col, pay_ref, head_ref, col_ref, row_ref, sems):
+        self.n_row, self.n_col = n_row, n_col
+        self.pay, self.head, self.col, self.row = pay_ref, head_ref, col_ref, row_ref
+        (self.local, self.hsend, self.qrecv, self.hrecv, self.csend, self.crecv, self.xsend, self.xrecv, self.rsend, self.rrecv) = sems
+        self.r, self.c = lax.axis_index("row"), lax.axis_index("col")
+        self.x, self.z = self.r // NZ, self.r % NZ
+        self.ny = n_col // 2
+        self.y, self.core = self.c // 2, self.c % 2
+        self.rays = pay_ref.shape[0]
+        self.part = self.rays // QUARTERS
+        self.sends = []
+
+    def at_row(self, x, z):
+        return (x * NZ + z, self.c)
+
+    def at_col(self, y, core):
+        return (self.r, y * 2 + core)
+
+    def barrier(self):
+        sem = pltpu.get_barrier_semaphore()
+        for d in range(1, NX):
+            pl.semaphore_signal(sem, inc=1, device_id=self.at_row((self.x + d) % NX, self.z), device_id_type=MESH)
+        for d in range(1, NZ):
+            pl.semaphore_signal(sem, inc=1, device_id=self.at_row(self.x, (self.z + d) % NZ), device_id_type=MESH)
+        for d in range(1, self.n_col):
+            pl.semaphore_signal(sem, inc=1, device_id=(self.r, (self.c + d) % self.n_col), device_id_type=MESH)
+        pl.semaphore_wait(sem, NX + NZ + self.n_col - 3)
+
+    def quarter(self, b, q, device, send):
+        where = self.head.at[b * self.n_col + self.c, pl.ds(pl.multiple_of(q * self.part, self.part), self.part)]
+        return remote(where, where, self.hsend.at[send], self.qrecv.at[b * QUARTERS + q], device)
+
+    def block(self, b, col, device, send):
+        where = self.head.at[b * self.n_col + col]
+        return remote(where, where, self.hsend.at[send], self.hrecv.at[b * self.n_col + col], device)
+
+    def send(self, copy, when=None):
+        self.sends.append((copy, when))
+        if when is None:
+            copy.start()
+        else:
+            pl.when(when)(copy.start)
+
+    def gather_head(self):
+        x, y, z, c, core = self.x, self.y, self.z, self.c, self.core
+        here = self.at_row(x, z)
+        source = [(x == 0) & (z == b) for b in range(2)]
+        for b in range(2):
+            @pl.when(source[b])
+            def _(b=b):
+                self.head[b * self.n_col + c] = self.pay[...]
+
+        count = 0
+        for b in range(2):
+            for q in range(1, QUARTERS):
+                self.send(self.quarter(b, q, self.at_row(q, z), count + q - 1), source[b])
+        count += QUARTERS - 1
+        onward = jnp.where((z >= 1) & (z <= 3), z + 1, (z + NZ - 1) % NZ)
+        for b in range(2):
+            pl.when(jnp.logical_not(source[b]))(self.quarter(b, x, here, 0).wait_recv)
+            self.send(self.quarter(b, x, self.at_row(x, onward), count), (z != 4) & (z != 5))
+            self.send(self.quarter(b, x, self.at_row(x, 1 - b), count + 1), z == b)
+            for d in range(1, NX):
+                to = (x + d) % NX
+                self.send(self.quarter(b, x, self.at_row(to, z), count + 1 + d), jnp.logical_not((to == 0) & (z == b)))
+            count += 1 + NX
+        left, right, across = (y + self.ny - 1) % self.ny, (y + 1) % self.ny, (y + 2) % self.ny
+        for b in range(2):
+            for d in range(1, NX):
+                pl.when(jnp.logical_not(source[b]))(self.quarter(b, (x + d) % NX, here, 0).wait_recv)
+            self.send(self.block(b, c, self.at_col(right, core), count))
+            self.send(self.block(b, c, self.at_col(left, core), count + 1))
+            self.send(self.block(b, c, self.at_col(y, 1 - core), count + 2))
+            count += 3
+        self.start_columns()
+        for b in range(2):
+            for near, far, relay in ((left, right, b == 0), (right, left, b == 1)):
+                came = near * 2 + core
+                self.block(b, came, here, 0).wait_recv()
+                if relay:
+                    self.send(self.block(b, came, self.at_col(far, core), count))
+                    count += 1
+                self.send(self.block(b, came, self.at_col(y, 1 - core), count))
+                count += 1
+        for b in range(2):
+            came = across * 2 + core
+            self.block(b, came, here, 0).wait_recv()
+            self.send(self.block(b, came, self.at_col(y, 1 - core), count))
+            count += 1
+        self.start_rows()
+        for b in range(2):
+            for d in range(self.ny):
+                self.block(b, ((y + d) % self.ny) * 2 + 1 - core, here, 0).wait_recv()
+
+    def column(self, z, d):
+        return remote(
+            self.pay, self.col.at[self.x * NZ + z], self.csend.at[d], self.crecv.at[z], self.at_row(self.x, (self.z + d) % NZ)
         )
 
-    def to_cols(d, src_col):
-        return pltpu.make_async_remote_copy(
-            src_ref=pay_ref,
-            dst_ref=row_ref.at[src_col],
-            send_sem=rsend.at[d],
-            recv_sem=rrecv.at[src_col],
-            device_id=(r, lax.rem(c + d, n_col)),
-            device_id_type=MESH,
-        )
-
-    def head_to_cols(d, src_col):
-        return pltpu.make_async_remote_copy(
-            src_ref=col_ref.at[pl.ds(0, 2)],
-            dst_ref=head_ref.at[:, pl.ds(pl.multiple_of(src_col * rays, rays), rays)],
-            send_sem=hsend.at[d],
-            recv_sem=hrecv.at[src_col],
-            device_id=(r, lax.rem(c + d, n_col)),
-            device_id_type=MESH,
-        )
-
-    @pl.when(r < 2)
-    def _():
-        for d in range(1, n_row):
-            to_rows(d, r).start()
-
-    own = pltpu.make_async_copy(pay_ref, col_ref.at[r], local_sem.at[0])
-    own.start()
-    own_row = pltpu.make_async_copy(pay_ref, row_ref.at[c], local_sem.at[1])
-    own_row.start()
-    own.wait()
-    for s in range(2):
-        @pl.when(r != s)
-        def _(s=s):
-            to_rows(1, s).wait_recv()
-
-    for d in range(1, n_col):
-        head_to_cols(d, c).start()
-    own_head = pltpu.make_async_copy(
-        col_ref.at[pl.ds(0, 2)], head_ref.at[:, pl.ds(pl.multiple_of(c * rays, rays), rays)], local_sem.at[2]
-    )
-    own_head.start()
-
-    @pl.when(r >= 2)
-    def _():
-        for d in range(1, n_row):
-            to_rows(d, r).start()
-
-    for d in range(1, n_col):
-        to_cols(d, c).start()
-
-    own_row.wait()
-    own_head.wait()
-    for d in range(1, n_col):
-        head_to_cols(d, lax.rem(c + d, n_col)).wait_recv()
-        to_cols(d, lax.rem(c + d, n_col)).wait_recv()
-    for s in range(2, n_row):
-        @pl.when(r != s)
-        def _(s=s):
-            to_rows(1, s).wait_recv()
-    for d in range(1, n_col):
-        head_to_cols(d, c).wait_send()
-        to_cols(d, c).wait_send()
-    for d in range(1, n_row):
-        to_rows(d, r).wait_send()
-
-
-def gather(payload, n_row, n_col):
-    rays, width = payload.shape
-    dma = pltpu.SemaphoreType.DMA
-    return pl.pallas_call(
-        functools.partial(gather_kernel, n_row, n_col),
-        out_shape=(
-            jax.ShapeDtypeStruct((n_row, rays, width), BF16),
-            jax.ShapeDtypeStruct((n_col, rays, width), BF16),
-            jax.ShapeDtypeStruct((2, n_col * rays, width), BF16),
-        ),
-        in_specs=[ANY],
-        out_specs=(ANY, ANY, ANY),
-        scratch_shapes=[
-            dma((3,)), dma((n_row,)), dma((n_row,)), dma((n_col,)), dma((n_col,)), dma((n_col,)), dma((n_col,)),
-        ],
-        compiler_params=pltpu.CompilerParams(collective_id=0, has_side_effects=True),
-        name="gather_features",
-    )(payload)
+    def plane(self, x, d):
+        where = self.col.at[pl.ds(pl.multiple_of(x * NZ, NZ), NZ)]
+        return remote(where, where, self.xsend.at[d], self.xrecv.at[x], self.at_row((self.x + d) % NX, self.z))
+
+    def across_row(self, col, d):
+        return remote(self.pay, self.row.at[col], self.rsend.at[d], self.rrecv.at[col], (self.r, (self.c + d) % self.n_col))
+
+    def start_columns(self):
+        self.own_col = pltpu.make_async_copy(self.pay, self.col.at[self.r], self.local.at[0])
+        self.own_col.start()
+        for d in range(1, NZ):
+            self.column(self.z, d).start()
+
+    def start_rows(self):
+        self.own_row = pltpu.make_async_copy(self.pay, self.row.at[self.c], self.local.at[1])
+        self.own_row.start()
+        for d in range(1, self.n_col):
+            self.across_row(self.c, d).start()
+
+    def start_planes(self):
+        self.own_col.wait()
+        for d in range(1, NZ):
+            self.column((self.z + d) % NZ, d).wait_recv()
+        for d in range(1, NX):
+            self.plane(self.x, d).start()
+
+    def finish(self):
+        self.own_row.wait()
+        for d in range(1, self.n_col):
+            self.across_row((self.c + d) % self.n_col, d).wait_recv()
+        for d in range(1, NX):
+            self.plane((self.x + d) % NX, d).wait_recv()
+        for copy, when in self.sends:
+            if when is None:
+                copy.wait_send()
+            else:
+                pl.when(when)(copy.wait_send)
+        for d in range(1, NZ):
+            self.column(self.z, d).wait_send()
+        for d in range(1, NX):
+            self.plane(self.x, d).wait_send()
+        for d in range(1, self.n_col):
+            self.across_row(self.c, d).wait_send()
 
 
 def table():
@@ -212,7 +260,7 @@
             d_ref[W * m : W * m + W, :] = total
 
 
-def head_kernel(head_ref, uhi_ref, ulo_ref, whi_ref, wlo_ref, s_ref, w_ref, d_ref):
+def factor_head(head_ref, uhi_ref, ulo_ref, whi_ref, wlo_ref, s_ref, w_ref, d_ref, midway):
     n = HEAD // B
     feat = head_ref[:, : head_ref.shape[1] - EXTRA]
     extra = head_ref[:, head_ref.shape[1] - EXTRA :]
@@ -249,7 +297,9 @@
         lax.switch(j, [tail(i) for i in range(n)])
         return carry
 
-    lax.fori_loop(0, n, step, 0)
+    lax.fori_loop(0, 2, step, 0)
+    midway()
+    lax.fori_loop(2, n, step, 0)
     for p in range(PANELS):
         a, b = w_ref[2 * p], w_ref[2 * p + 1]
         low = -nn(b, tn(s_ref[PANEL * p : PANEL * p + B, PANEL * p + B : PANEL * p + PANEL], a, HIGHEST), HIGHEST)
@@ -259,21 +309,47 @@
         wlo_ref[p, :B, B:] = jnp.zeros((B, B), BF16)
 
 
-def factor_head(head):
+def head_kernel(n_row, n_col, pay_ref, col_ref, row_ref, out_head_ref, uhi_ref, ulo_ref, whi_ref, wlo_ref, blocks_ref, head_ref, s_ref, w_ref, d_ref, *sems):
+    feed = Feed(n_row, n_col, pay_ref, blocks_ref, col_ref, row_ref, sems)
+    feed.barrier()
+    feed.gather_head()
+    rays = feed.rays
+    for i in range(HEAD // rays):
+        head_ref[i * rays : i * rays + rays, :] = blocks_ref[i]
+    out = pltpu.make_async_copy(head_ref, out_head_ref, feed.local.at[2])
+    out.start()
+    factor_head(head_ref, uhi_ref, ulo_ref, whi_ref, wlo_ref, s_ref, w_ref, d_ref, feed.start_planes)
+    feed.finish()
+    out.wait()
+
+
+def gather_and_factor(payload, n_row, n_col):
+    rays, width = payload.shape
+    dma = pltpu.SemaphoreType.DMA
     return pl.pallas_call(
-        head_kernel,
+        functools.partial(head_kernel, n_row, n_col),
         out_shape=(
+            jax.ShapeDtypeStruct((n_row, rays, width), BF16),
+            jax.ShapeDtypeStruct((n_col, rays, width), BF16),
+            jax.ShapeDtypeStruct((HEAD, width), BF16),
             jax.ShapeDtypeStruct((HEAD, HEAD), BF16),
             jax.ShapeDtypeStruct((HEAD, HEAD), BF16),
             jax.ShapeDtypeStruct((PANELS, PANEL, PANEL), BF16),
             jax.ShapeDtypeStruct((PANELS, PANEL, PANEL), BF16),
         ),
         in_specs=[VMEM],
-        out_specs=(VMEM,) * 4,
-        scratch_shapes=[pltpu.VMEM((HEAD, HEAD), F32), pltpu.VMEM((HEAD // B, B, B), F32), pltpu.VMEM((B, B), F32)],
-        compiler_params=pltpu.CompilerParams(vmem_limit_bytes=40 << 20),
-        name="factor_head",
-    )(head)
+        out_specs=(ANY, ANY, ANY, VMEM, VMEM, VMEM, VMEM),
+        scratch_shapes=[
+            pltpu.VMEM((HEAD // rays, rays, width), BF16),
+            pltpu.VMEM((HEAD, width), BF16),
+            pltpu.VMEM((HEAD, HEAD), F32),
+            pltpu.VMEM((HEAD // B, B, B), F32),
+            pltpu.VMEM((B, B), F32),
+            dma((3,)), dma((32,)), dma((2 * QUARTERS,)), dma((2 * n_col,)), dma((NZ,)), dma((NZ,)), dma((NX,)), dma((NX,)), dma((n_col,)), dma((n_col,)),
+        ],
+        compiler_params=pltpu.CompilerParams(collective_id=0, has_side_effects=True, vmem_limit_bytes=40 << 20),
+        name="gather_and_factor",
+    )(payload)
 
 
 def front_kernel(row_ref, head_ref, col_ref, uhi_ref, ulo_ref, whi_ref, wlo_ref, front_ref, factor_ref, tab_ref, hhot_ref, rval_ref, rhi_ref, rlo_ref, hi_ref, lo_ref):
@@ -351,17 +427,16 @@
     n_row, n_col = lax.axis_size("row"), lax.axis_size("col")
     rays = noise.shape[0]
     lanes = jnp.arange(EXTRA, dtype=jnp.int32)[None, :]
-    hi = noise.astype(BF16).astype(F32)
-    mid = (noise - hi).astype(BF16).astype(F32)
+    hi = lax.reduce_precision(noise, 8, 7)
+    mid = lax.reduce_precision(noise - hi, 8, 7)
     low = noise - hi - mid
     extra = jnp.where(lanes == slot_of_ray[:, None], 1.0, 0.0)
     for i, part in enumerate((hi, mid, low)):
         extra = jnp.where(lanes == NT + i, part[:, None], extra)
     payload = jnp.concatenate([features, extra.astype(BF16)], axis=1)
     width = payload.shape[1]
-    col, row, head = gather(payload, n_row, n_col)
-    col, row, head = col.reshape(n_row * rays, width), row.reshape(n_col * rays, width), head.reshape(HEAD, width)
-    return front_and_factor(row, head, col, *factor_head(head))
+    col, row, head, *factors = gather_and_factor(payload, n_row, n_col)
+    return front_and_factor(row.reshape(n_col * rays, width), head, col.reshape(n_row * rays, width), *factors)
 
 
 def solution(mesh):

time: 220 us -> 136 us (0.62)
  the two profiles are of different devices: /device:TPU:86 before, /device:TPU:161 now
where the time goes in v2:
time: 136 us; the launch traced here: 135 us
  Pallas kernels  125 us (92%)
  local copies, waits for them, and re-layouts  7.82 us (6%)
  other arithmetic  2.27 us (2%)
    pallas_call x1, Pallas kernels, gather_and_factor(): pl.pallas_call(functools.partial(head_kernel, n_row, n_col), out_shape=(j...  87.4 us
    pallas_call x1, Pallas kernels, front_and_factor(): pl.pallas_call(front_kernel, grid=(cols // tile,), out_shape=(jax.ShapeDt...  37.2 us
    unnamed x14, local copies, waits for them, and re-layouts  7.82 us

profile of v2, /device:TPU:161, one launch (start us, length us, event | category | flops | bytes accessed | tf_op | source)
XLA Modules:
  0.0 135.4 jit_solution(17367317915698640527)
XLA Ops:
  0.7 0.7 reduce-precision_subtract_fusion
  1.3 0.7 select_convert_fusion
  2.1 0.8 pad_maximum_fusion.pay_ref
  2.9 87.4 %gather_and_factor.1 = (bf16[32,64,640]{2,1,0:T(8,128)(2,1)S(1)}, bf16[8,64,640]{2,1,0:T(8,128)(2,1)S(1)}, bf16[1024,640]{1,0:T(8,128)(2,1)S(1)}, bf16[1024,1024...) custom-call(bf16[64,640]{1,0:T(8,128)(2,1)S(1)} %pad_maximum_fusion., ...), custom_call_target="tpu_custom_call" | custom-call | tf_op jit(solution)/shard_map/gather_and_factor/pallas_call | solution.py:329
  90.4 0.0 copy-start
  90.4 1.5 %copy-done = bf16[32,64,640]{2,1,0:T(8,128)(2,1)} copy-done((bf16[32,64,640]{2,1,0:T(8,128)(2,1)}, bf16[32,64,640]{2,1,0:T(8,128)(2,1)S(1)}, u32[]{:S(2)}) %copy-start) | copy-done | bytes 2621464
  91.9 0.0 copy-start.1
  91.9 1.3 copy-done.1
  93.2 0.0 copy-start.2
  93.2 1.4 %copy-done.2 = bf16[1024,1024]{1,0:T(8,128)(2,1)} copy-done((bf16[1024,1024]{1,0:T(8,128)(2,1)}, bf16[1024,1024]{1,0:T(8,128)(2,1)S(1)}, u32[]{:S(2)}) %copy-start.2) | copy-done | bytes 2097176
  94.6 0.0 copy-start.3
  94.6 1.1 copy-done.3
  95.6 0.0 copy-start.4
  95.6 0.9 copy-done.4
  96.5 0.0 copy-start.5
  96.5 0.8 copy-done.5
  97.4 0.0 copy-start.6
  97.4 0.8 copy-done.6
  98.2 37.2 %front_and_factor.1 = (f32[512,1,2048]{2,1,0:T(1,128)}, f32[512,1024]{1,0:T(8,128)}) custom-call(bf16[512,640]{1,0:T(8,128)(2,1)} %bitcast.3, bf16[1024,640]{1,0:T(8,128)(2,1)} %copy-done.3, bf16[2048,640]{1,0:T(8,128)(2,1)} %bitcast.2, bf16[1024,1024]{1,0:T(8,128)(2,1)} %copy-done.1, bf16[1024,1024]{1,0:T(8,128)(2,1)} %copy-done.2, ...), custom_call_target="tpu_custom_call" | custom-call | tf_op jit(solution)/shard_map/front_and_factor/pallas_call | solution.py:406
  (2 shorter events, 0.0 us)
Async XLA Ops:
  90.4 1.5 %copy-start = (bf16[32,64,640]{2,1,0:T(8,128)(2,1)}, bf16[32,64,640]{2,1,0:T(8,128)(2,1)S(1)}, u32[]{:S(2)}) copy-start(bf16[32,64,640]{2,1,0:T(8,128)(2,1)S(1)} %get-tuple-element.11) | copy-start | bytes 7864324
  91.9 1.3 copy-start.1
  93.2 1.4 %copy-start.2 = (bf16[1024,1024]{1,0:T(8,128)(2,1)}, bf16[1024,1024]{1,0:T(8,128)(2,1)S(1)}, u32[]{:S(2)}) copy-start(bf16[1024,1024]{1,0:T(8,128)(2,1)S(1)} %get-tuple-element.13.ulo_ref) | copy-start | bytes 6291460
  94.6 1.1 copy-start.3
  95.6 0.9 copy-start.4
  96.5 0.8 copy-start.5
  97.4 0.8 copy-start.6
